TPU v7x, 128 devices: a whole 4x4x4 slice. The times are simulated.
128 devices in a mesh: tile: 64 (over y, z, x), chan: 2 (over core).
Axes of the slice: x: 4, y: 4, z: 4, core: 2. Of those that a mesh axis runs over, the one named last changes fastest.
Arguments:
- attributes: bfloat16 [35, 1024, 512], P(None, 'tile'), may hold values from -6 to 6
- cell_basin: int32 [1024, 512], P('tile'), may hold values from 0 to 8191, as said below
- basin_cells: int32 [8192], P('tile'), may hold values from 1 to 127, as said below
- conv_first: bfloat16 [128, 3, 3, 35], P('chan'), may hold values from -0.5 to 0.5
- conv_second: bfloat16 [128, 3, 3, 128], P('chan'), may hold values from -0.25 to 0.25
- conv_third: bfloat16 [128, 3, 3, 128], P('chan'), may hold values from -0.25 to 0.25
- head_weight: bfloat16 [128, 12], P('chan'), may hold values from -0.75 to 0.75
- precip: float32 [30, 16, 8192], P(None, 'chan', 'tile'), may hold values from 0 to 250
- temp: float32 [30, 16, 8192], P(None, 'chan', 'tile'), may hold values from -24 to 24
- pet: float32 [30, 16, 8192], P(None, 'chan', 'tile'), may hold values from 0.5 to 4
Outputs:
- streamflow: float32 [30, 16, 8192], P(None, 'chan', 'tile')
Inputs may be any that keep to these rules, and one draw needn't show every extreme that they name: `cell_basin`: in each tile the 8192 cells in row-major order form 64 runs of 128 cells; the runs of one tile go to 64 different owners, so that every owner receives exactly 128 cells from every tile. The basins of owner o are o * 128 to o * 128 + 127; one run holds 2 whole basins, each a contiguous part of the run. `basin_cells`: the number of cells of cell_basin in each basin; some basin reaches the most.
All inputs are finite; a program needn't handle non-finite values.
Results may differ from a plain program's by a relative error of at most 0.00061.
Values may be sent and summed in bfloat16 or wider, within the bound.
A program may use at most 64 MiB of HBM per device.

v0:
```python
import jax
import jax.numpy as jnp
from jax import lax
from jax.sharding import PartitionSpec as P

LAGS = 15
LOW = [-2.0, 0.5, 50.0, 1.0, 0.3, 0.05, 0.01, 0.001, 0.0, 0.5, 1.0, 0.5]
SPAN = [4.0, 5.5, 450.0, 4.0, 0.7, 0.45, 0.29, 0.099, 50.0, 5.5, 2.0, 2.5]


def padded_2(cells, sides, width):
    for axis, dim in sides:
        count = lax.axis_size(axis)
        ends = count - 1
        head = lax.slice_in_dim(cells, 0, width, axis=dim)
        tail = lax.slice_in_dim(cells, cells.shape[dim] - width, cells.shape[dim], axis=dim)
        cells = jnp.concatenate(
            [
                lax.ppermute(tail, axis, [(i, (i + 1) % count) for i in range(ends)]),
                cells,
                lax.ppermute(head, axis, [((i + 1) % count, i) for i in range(ends)]),
            ],
            axis=dim,
        )
    return cells


def pad_columns(field):
    return jnp.pad(field, ((0, 0), (0, 0), (1, 1)))


def conv_taps(total, weight, padded):
    height = total.shape[1]
    width = total.shape[2]
    for row_tap in range(3):
        for col_tap in range(3):
            taps = weight[:, row_tap, col_tap, :]
            window = padded[:, row_tap : row_tap + height, col_tap : col_tap + width]
            total = total + jnp.einsum(
                "oc,chw->ohw", taps, window, preferred_element_type=jnp.float32
            )
    return total


def bucket_run(param, precip, temp, pet):
    tt, cfmax, fc, beta, lp = (param[0], param[1], param[2], param[3], param[4])
    k0, k1, k2, uzl, perc = (param[5], param[6], param[7], param[8], param[9])

    def day(state, force):
        snow, soil, upper, lower = state
        rain_in, air, demand = force
        liquid = jax.nn.sigmoid(air - tt)
        gained = snow + rain_in * (1.0 - liquid)
        snow_new = jnp.maximum(gained - cfmax * jnp.maximum(air - tt, 0.0), 0.0)
        melt = gained - snow_new
        inflow = rain_in * liquid + melt
        recharge = inflow * jnp.power(soil / fc, beta)
        soil = soil + inflow - recharge
        excess = jnp.maximum(soil - fc, 0.0)
        soil = soil - excess
        soil = jnp.where(soil < lp * fc, soil * (1.0 - demand / (lp * fc)), soil - demand)
        upper = upper + recharge + excess
        upper_new = jnp.maximum(upper - perc, 0.0)
        lower = lower + upper - upper_new
        quick = k0 * jnp.maximum(upper_new - uzl, 0.0)
        slow = k1 * upper_new
        upper = upper_new - quick - slow
        base = k2 * lower
        lower = lower - base
        return ((snow_new, soil, upper, lower), quick + slow + base)

    shape = precip.shape[1:]
    start = (
        jnp.zeros(shape, jnp.float32),
        jnp.broadcast_to(0.5 * fc, shape),
        jnp.full(shape, 5.0, jnp.float32),
        jnp.full(shape, 20.0, jnp.float32),
    )
    final, runoff = lax.scan(day, start, (precip, temp, pet))
    return runoff


def route(param, runoff):
    days = runoff.shape[0]
    lag = jnp.arange(LAGS).astype(jnp.float32) + 0.5
    weight = jnp.exp(
        (param[10] - 1.0)[None, :] * jnp.log(lag)[:, None] - lag[:, None] / param[11][None, :]
    )
    weight = weight / jnp.sum(weight, axis=0, keepdims=True)
    later = jnp.arange(days)[:, None] - jnp.arange(days)[None, :]
    pick = (later[None, :, :] == jnp.arange(LAGS)[:, None, None]).astype(jnp.float32)
    matrix = jnp.einsum("kts,kb->tsb", pick, weight, precision=lax.Precision.HIGHEST)
    return jnp.einsum("tsb,swb->twb", matrix, runoff, precision=lax.Precision.HIGHEST)


def on_device(
    attributes,
    cell_basin,
    basin_cells,
    conv_first,
    conv_second,
    conv_third,
    head_weight,
    precip,
    temp,
    pet,
):
    height = attributes.shape[1]
    width = attributes.shape[2]
    n_chan = lax.axis_size("chan")
    owners = lax.axis_size("tile")
    half = height // n_chan
    rimmed = padded_2(attributes, (("tile", 1),), 1)
    empty = jnp.zeros((conv_first.shape[0], height, width), jnp.float32)
    first = conv_taps(empty, conv_first, pad_columns(rimmed))
    hidden = jnp.maximum(first, 0.0).astype(jnp.bfloat16)
    for weight in (conv_second, conv_third):
        rim = padded_2(hidden, (("tile", 1),), 1)
        total = conv_taps(
            empty, weight, pad_columns(lax.all_gather(rim, "chan", axis=0, tiled=True))
        )
        hidden = jnp.maximum(total, 0.0).astype(jnp.bfloat16)
    raw = lax.psum_scatter(
        jnp.einsum("cp,chw->hpw", head_weight, hidden, preferred_element_type=jnp.float32),
        "chan",
        scatter_dimension=0,
        tiled=True,
    )
    params_count = raw.shape[1]
    share = jnp.transpose(jax.nn.sigmoid(raw), (1, 0, 2)).reshape(params_count, -1)
    mine = lax.dynamic_slice_in_dim(cell_basin, lax.axis_index("chan") * half, half, 0).reshape(-1)
    basins_here = basin_cells.shape[0]
    sums = jax.ops.segment_sum(share.T, mine, num_segments=owners * basins_here)
    sums = sums.T.reshape(params_count, owners, basins_here)
    arrived = lax.all_to_all(sums, "tile", split_axis=1, concat_axis=1, tiled=True)
    partial_value = jnp.sum(arrived, axis=1)
    total_sum = lax.psum(partial_value, "chan")
    mean = total_sum / basin_cells.astype(jnp.float32)[None, :]
    param = jnp.array(LOW, jnp.float32)[:, None] + jnp.array(SPAN, jnp.float32)[:, None] * mean
    runoff = bucket_run(param, precip, temp, pet)
    return route(param, runoff)


def solution(mesh):
    return jax.shard_map(
        on_device,
        mesh=mesh,
        in_specs=(
            P(None, "tile", None),
            P("tile", None),
            P("tile"),
            P("chan", None, None, None),
            P("chan", None, None, None),
            P("chan", None, None, None),
            P("chan", None),
            P(None, "chan", "tile"),
            P(None, "chan", "tile"),
            P(None, "chan", "tile"),
        ),
        out_specs=P(None, "chan", "tile"),
        check_vma=False,
    )
```

profile of v0, /device:TPU:1, one launch (start us, length us, event | category | flops | bytes accessed | tf_op | source)
XLA Modules:
  0.0 255.4 jit_solution(3265855978443713015)
XLA Ops:
  6.5 1.4 copy.77
  7.9 3.9 %collective-permute-start = (bf16[35,1,512]{2,0,1:T(8,128)(2,1)S(1)}, bf16[35,1,512]{2,0,1:T(8,128)(2,1)S(1)}, u32[]{:S(2)}, u32[]{:S(2)}) collective-permute-start(bf16[35,1,512]{2,0,1:T(8,128)(2,1)S(1)} %get-tuple-element.376), channel_id=1, source_target_pairs={{0,2},{2,4},{4,6},{6,8},{8,10},{10,12},{12,14},{14,16},{16,18},{18... | collective-permute-start | bytes 107528 | tf_op jit(solution)/shard_map/ppermute | solution.py:19
  11.9 1.4 collective-permute-start.1
  13.3 1.7 fusion.113
  15.1 1.7 collective-permute-done.1
  20.9 2.4 fusion.36
  23.3 3.2 %collective-permute-start.2 = (bf16[64,1,512]{2,0,1:T(8,128)(2,1)S(1)}, bf16[64,1,512]{2,0,1:T(8,128)(2,1)S(1)}, u32[]{:S(2)}, u32[]{:S(2)}) collective-permute-start(bf16[64,1,512]{2,0,1:T(8,128)(2,1)S(1)} %get-tuple-element.374), channel_id=1, source_target_pairs={{0,2},{2,4},{4,6},{6,8},{8,10},{10,12},{12,14},{14,16},{16,18},{18... | collective-permute-start | bytes 196616 | tf_op jit(solution)/shard_map/ppermute | solution.py:19
  26.6 1.3 collective-permute-start.3
  27.9 3.7 %collective-permute-done.3 = bf16[64,1,512]{2,0,1:T(8,128)(2,1)S(1)} collective-permute-done((bf16[64,1,512]{2,0,1:T(8,128)(2,1)S(1)}, bf16[64,1,512]{2,0,1:T(8,128)(2,1)S(1)}, u32[]{:S(2)}, u32[]{:S(2)}) %collective-permute-start.3) | collective-permute-done | bytes 65568 | tf_op jit(solution)/shard_map/ppermute | solution.py:21
  31.6 1.2 pad_maximum_fusion
  33.0 24.5 %all-gather.3.cloned.1.call-done = bf16[128,18,512]{2,0,1:T(8,128)(2,1)} async-done(((bf16[64,18,512]{2,0,1:T(8,128)(2,1)}), bf16[128,18,512]{2,0,1:T(8,128)(2,1)}) %all-gather.3.cloned.1.call-update) | async-done | bytes 2359312 | tf_op jit(solution)/shard_map/all_gather | solution.py:120
  57.5 2.5 fusion.11
  60.1 0.8 fusion.12
  60.9 0.8 fusion.13
  61.6 0.8 fusion.14
  62.4 0.8 fusion.15
  64.5 1.5 fusion.40
  66.1 3.3 %collective-permute-start.4 = (bf16[64,1,512]{2,0,1:T(8,128)(2,1)S(1)}, bf16[64,1,512]{2,0,1:T(8,128)(2,1)S(1)}, u32[]{:S(2)}, u32[]{:S(2)}) collective-permute-start(bf16[64,1,512]{2,0,1:T(8,128)(2,1)S(1)} %get-tuple-element.372), channel_id=1, source_target_pairs={{0,2},{2,4},{4,6},{6,8},{8,10},{10,12},{12,14},{14,16},{16,18},{18... | collective-permute-start | bytes 196616 | tf_op jit(solution)/shard_map/ppermute | solution.py:19
  69.4 1.3 collective-permute-start.5
  70.7 3.7 %collective-permute-done.5 = bf16[64,1,512]{2,0,1:T(8,128)(2,1)S(1)} collective-permute-done((bf16[64,1,512]{2,0,1:T(8,128)(2,1)S(1)}, bf16[64,1,512]{2,0,1:T(8,128)(2,1)S(1)}, u32[]{:S(2)}, u32[]{:S(2)}) %collective-permute-start.5) | collective-permute-done | bytes 65568 | tf_op jit(solution)/shard_map/ppermute | solution.py:21
  74.4 1.2 pad_maximum_fusion.1
  75.9 19.4 %all-gather.5.cloned.1.call-done = bf16[128,18,512]{2,0,1:T(8,128)(2,1)} async-done(((bf16[64,18,512]{2,0,1:T(8,128)(2,1)}), bf16[128,18,512]{2,0,1:T(8,128)(2,1)}) %all-gather.5.cloned.1.call-update) | async-done | bytes 2359312 | tf_op jit(solution)/shard_map/all_gather | solution.py:120
  95.3 3.9 %fusion.17 = f32[16,512,64]{1,2,0:T(8,128)} fusion(bf16[128,18,512]{2,0,1:T(8,128)(2,1)} %all-gather.5.cloned.1.call-done, bf16[64,3,3,128]{3,0,2,1:T(8,128)(2,1)S(1)} %copy-done.3), kind=kOutput, calls=%fused_computation.49 | convolution fusion | flops 134217728 | bytes 4472832 | tf_op jit(solution)/shard_map/oc,chw->ohw/dot_general | solution.py:39
  99.2 2.1 fusion.18
  101.3 2.2 fusion.19
  103.4 2.2 fusion.20
  105.6 2.1 fusion.21
  107.8 1.8 fusion.23
  109.5 1.7 fusion.25
  111.3 1.7 fusion.27
  113.0 8.3 %fusion.43 = f32[16,12,512]{2,1,0:T(8,128)} fusion(bf16[128,18,512]{2,0,1:T(8,128)(2,1)S(1)} %copy-done.1, f32[16,512,64]{1,2,0:T(8,128)} %fusion.23, f32[16,512,64]{1,2,0:T(8,128)} %fusion.21, f32[16,512,64]{1,2,0:T(8,128)} %fusion.20, f32[16,512,64]{1,2,0:T(8,128)} %fusion.25, f32[16,512,64]{1,2,0:T(8,128)} %fusion.19, f32[16,512,64]{1,2,0:T(8,128)} %fusion.18, ...), kind=kOutput, calls=%fused_computation.83 | convolution fusion | flops 152043520 | bytes 19550208 | tf_op jit(solution)/shard_map/cp,chw->hpw/dot_general | solution.py:124
  121.4 12.1 %reduce-scatter.2.cloned.1.call-done = f32[8,12,512]{2,1,0:T(8,128)} async-done(((f32[16,12,512]{2,1,0:T(8,128)}), f32[8,12,512]{2,1,0:T(8,128)}) %reduce-scatter.2.cloned.1.call-update) | async-done | bytes 196624 | tf_op jit(solution)/shard_map/reduce_scatter | solution.py:123
  133.4 1.0 divide_bitcast_fusion
  135.4 30.7 %scatter_custom_fusion = f32[8192,12]{1,0:T(8,128)} fusion(s32[4096]{0:T(1024)S(1)} %bitcast.289, f32[4096,12]{1,0:T(8,128)S(1)} %copy.84, f32[]{:T(128)} %constant.50.clone.1), kind=kCustom, calls=%fused_computation.76 | custom fusion | flops 49152 | bytes 393220 | tf_op jit(solution)/shard_map/scatter-add | solution.py:133
  166.2 3.6 %copy.85 = f32[12,64,128]{2,0,1:T(8,128)} copy(f32[12,64,128]{0,2,1:T(8,128)} %bitcast.269) | data formatting | bytes 786432 | tf_op jit(solution)/shard_map/reshape | solution.py:134
  169.8 10.1 %all-to-all-start = ((f32[12,64,128]{2,0,1:T(8,128)}), f32[12,64,128]{2,0,1:T(8,128)S(1)}, u32[]{:S(2)}, u32[]{:S(2)}) async-start(f32[12,64,128]{2,0,1:T(8,128)} %copy.85), calls=%async_computation.1 | async-start | bytes 1048576 | tf_op jit(solution)/shard_map/all_to_all | solution.py:135
  180.0 12.6 %all-to-all-done = f32[12,64,128]{2,0,1:T(8,128)S(1)} async-done(((f32[12,64,128]{2,0,1:T(8,128)}), f32[12,64,128]{2,0,1:T(8,128)S(1)}, u32[]{:S(2)}, u32[]{:S(2)}) %all-to-all-start) | async-done | bytes 393248 | tf_op jit(solution)/shard_map/all_to_all | solution.py:135
  192.7 3.8 %psum.7 = f32[12,128]{1,0:T(8,128)S(1)} all-reduce(f32[12,128]{1,0:T(8,128)S(1)} %reduce_sum.18), channel_id=1, replica_groups=mesh['tile'=64,'chan'=2] {'chan'}, use_global_device_ids=true, to_apply=%region_3.4 | all-reduce | flops 1536 | bytes 12288 | tf_op jit(solution)/shard_map/psum | solution.py:137
  197.4 1.9 copy.89
  199.3 45.1 %while.21 = (s32[]{:T(128)}, f32[8,128]{1,0:T(8,128)S(1)}, f32[8,128]{1,0:T(8,128)S(1)}, f32[8,128]{1,0:T(8,128)S(1)}, f32[8,128]{1,0:T(8,128)S(1)}, /*index=5*/...) while((s32[]{:T(128)}, f32[8,128]{1,0:T(8,128)S(1)}, ...), condition=%wide.region_5.6_spmd.clone, body=%wide.region_4.5_spmd.clone.sunk | while | flops 63491 | bytes 82640 | solution.py:79
  223.3 0.8 fusion.166
  224.8 0.8 fusion.166
  226.3 0.8 fusion.166
  230.8 0.8 fusion.166
  232.3 0.8 fusion.166
  233.8 0.8 fusion.166
  244.6 3.4 %convolution_bitcast_fusion = f32[30,8,128]{0,1,2:T(8,128)S(1)} fusion(f32[30,8,128]{0,1,2:T(8,128)S(1)} %copy.88, f32[30,30,128]{1,0,2:T(8,128)S(1)} %copy.89), kind=kOutput, calls=%fused_computation.82 | convolution fusion | flops 11059200 | bytes 706560 | tf_op jit(solution)/shard_map/tsb,swb->twb/dot_general | solution.py:93
  248.0 0.9 copy.90
  (118 shorter events, 47.9 us)
Async XLA Ops:
  6.5 114.8 %copy-start = (s32[16,512]{1,0:T(8,128)S(1)}, s32[16,512]{1,0:T(8,128)}, u32[]{:S(2)}) copy-start(s32[16,512]{1,0:T(8,128)} %param.15) | copy-start | bytes 98308
  6.5 51.0 %all-gather.3.cloned.1.call-start = ((), (), s32[]{:S(2)}) async-start(), calls=%async_computation.2 | async-start | bytes 3538944 | tf_op jit(solution)/shard_map/all_gather | solution.py:120
  7.9 7.1 %collective-permute-start = (bf16[35,1,512]{2,0,1:T(8,128)(2,1)S(1)}, bf16[35,1,512]{2,0,1:T(8,128)(2,1)S(1)}, u32[]{:S(2)}, u32[]{:S(2)}) collective-permute-start(bf16[35,1,512]{2,0,1:T(8,128)(2,1)S(1)} %get-tuple-element.376), channel_id=1, source_target_pairs={{0,2},{2,4},{4,6},{6,8},{8,10},{10,12},{12,14},{14,16},{16,18},{18... | collective-permute-start | bytes 107528 | tf_op jit(solution)/shard_map/ppermute | solution.py:19
  11.9 5.4 %copy-start.5 = (bf16[64,3,3,35]{0,3,2,1:T(8,128)(2,1)S(1)}, bf16[64,3,3,35]{0,3,2,1:T(8,128)(2,1)}, u32[]{:S(2)}) copy-start(bf16[64,3,3,35]{0,3,2,1:T(8,128)(2,1)} %param.17) | copy-start | bytes 120964
  11.9 4.9 %collective-permute-start.1 = (bf16[35,1,512]{2,0,1:T(8,128)(2,1)S(1)}, bf16[35,1,512]{2,0,1:T(8,128)(2,1)S(1)}, u32[]{:S(2)}, u32[]{:S(2)}) collective-permute-start(bf16[35,1,512]{2,0,1:T(8,128)(2,1)S(1)} %get-tuple-element.377), channel_id=1, source_target_pairs={{2,0},{4,2},{6,4},{8,6},{10,8},{12,10},{14,12},{16,14},{18,16},{20... | collective-permute-start | bytes 107528 | tf_op jit(solution)/shard_map/ppermute | solution.py:21
  23.3 34.2 %copy-start.4 = (bf16[64,3,3,128]{3,0,2,1:T(8,128)(2,1)S(1)}, bf16[64,3,3,128]{3,0,2,1:T(8,128)(2,1)}, u32[]{:S(2)}) copy-start(bf16[64,3,3,128]{3,0,2,1:T(8,128)(2,1)} %param.18) | copy-start | bytes 442372
  23.3 4.6 %collective-permute-start.2 = (bf16[64,1,512]{2,0,1:T(8,128)(2,1)S(1)}, bf16[64,1,512]{2,0,1:T(8,128)(2,1)S(1)}, u32[]{:S(2)}, u32[]{:S(2)}) collective-permute-start(bf16[64,1,512]{2,0,1:T(8,128)(2,1)S(1)} %get-tuple-element.374), channel_id=1, source_target_pairs={{0,2},{2,4},{4,6},{6,8},{8,10},{10,12},{12,14},{14,16},{16,18},{18... | collective-permute-start | bytes 196616 | tf_op jit(solution)/shard_map/ppermute | solution.py:19
  26.6 5.0 %collective-permute-start.3 = (bf16[64,1,512]{2,0,1:T(8,128)(2,1)S(1)}, bf16[64,1,512]{2,0,1:T(8,128)(2,1)S(1)}, u32[]{:S(2)}, u32[]{:S(2)}) collective-permute-start(bf16[64,1,512]{2,0,1:T(8,128)(2,1)S(1)} %get-tuple-element.375), channel_id=1, source_target_pairs={{2,0},{4,2},{6,4},{8,6},{10,8},{12,10},{14,12},{16,14},{18,16},{20... | collective-permute-start | bytes 196616 | tf_op jit(solution)/shard_map/ppermute | solution.py:21
  32.8 62.5 %all-gather.5.cloned.1.call-start = ((), (), s32[]{:S(2)}) async-start(), calls=%async_computation.3 | async-start | bytes 3538944 | tf_op jit(solution)/shard_map/all_gather | solution.py:120
  57.5 2.5 copy-start.2
  66.0 29.3 %copy-start.3 = (bf16[64,3,3,128]{3,0,2,1:T(8,128)(2,1)S(1)}, bf16[64,3,3,128]{3,0,2,1:T(8,128)(2,1)}, u32[]{:S(2)}) copy-start(bf16[64,3,3,128]{3,0,2,1:T(8,128)(2,1)} %param.19) | copy-start | bytes 442372
  66.1 4.6 %collective-permute-start.4 = (bf16[64,1,512]{2,0,1:T(8,128)(2,1)S(1)}, bf16[64,1,512]{2,0,1:T(8,128)(2,1)S(1)}, u32[]{:S(2)}, u32[]{:S(2)}) collective-permute-start(bf16[64,1,512]{2,0,1:T(8,128)(2,1)S(1)} %get-tuple-element.372), channel_id=1, source_target_pairs={{0,2},{2,4},{4,6},{6,8},{8,10},{10,12},{12,14},{14,16},{16,18},{18... | collective-permute-start | bytes 196616 | tf_op jit(solution)/shard_map/ppermute | solution.py:19
  69.4 5.0 %collective-permute-start.5 = (bf16[64,1,512]{2,0,1:T(8,128)(2,1)S(1)}, bf16[64,1,512]{2,0,1:T(8,128)(2,1)S(1)}, u32[]{:S(2)}, u32[]{:S(2)}) collective-permute-start(bf16[64,1,512]{2,0,1:T(8,128)(2,1)S(1)} %get-tuple-element.373), channel_id=1, source_target_pairs={{2,0},{4,2},{6,4},{8,6},{10,8},{12,10},{14,12},{16,14},{18,16},{20... | collective-permute-start | bytes 196616 | tf_op jit(solution)/shard_map/ppermute | solution.py:21
  75.6 57.8 %reduce-scatter.2.cloned.1.call-start = ((), (), s32[]{:S(2)}) async-start(), calls=%async_computation.4 | async-start | bytes 786432 | tf_op jit(solution)/shard_map/reduce_scatter | solution.py:123
  95.3 3.9 %copy-start.1 = (bf16[128,18,512]{2,0,1:T(8,128)(2,1)S(1)}, bf16[128,18,512]{2,0,1:T(8,128)(2,1)}, u32[]{:S(2)}) copy-start(bf16[128,18,512]{2,0,1:T(8,128)(2,1)} %all-gather.5.cloned.1.call-done) | copy-start | bytes 7077892
  111.3 1.7 copy-start.6
  166.2 13.8 %copy-start.9 = (s32[128]{0:T(128)S(1)}, s32[128]{0:T(128)}, u32[]{:S(2)}) copy-start(s32[128]{0:T(128)} %param.16) | copy-start | bytes 1540
  166.2 30.4 %copy-start.7 = (f32[12]{0:T(128)S(1)}, f32[12]{0:T(128)}, u32[]{:S(2)}) copy-start(f32[12]{0:T(128)} %constant.60.clone) | copy-start | bytes 148
  166.2 30.4 %copy-start.8 = (f32[12]{0:T(128)S(1)}, f32[12]{0:T(128)}, u32[]{:S(2)}) copy-start(f32[12]{0:T(128)} %constant.61.clone) | copy-start | bytes 148
  169.8 22.9 %all-to-all-start = ((f32[12,64,128]{2,0,1:T(8,128)}), f32[12,64,128]{2,0,1:T(8,128)S(1)}, u32[]{:S(2)}, u32[]{:S(2)}) async-start(f32[12,64,128]{2,0,1:T(8,128)} %copy.85), calls=%async_computation.1 | async-start | bytes 1048576 | tf_op jit(solution)/shard_map/all_to_all | solution.py:135
Sparse Core Ops, SparseCore 0:
  32.9 24.5 all-gather.2
  75.8 19.4 all-gather.4
  121.4 11.9 reduce-scatter.1
where the time goes:
time: 259 us; the launch traced here: 255 us
  other arithmetic  79.3 us (31%)
  waiting for transfers between devices  77.8 us (30%)
  matrix products  46.1 us (18%)
  starting transfers between devices  25.1 us (10%)
  between operations  13.5 us (5%)
  local copies, waits for them, and re-layouts  9.06 us (3%)
  blocking collectives  3.81 us (1%)
    all_gather x2, waiting for transfers between devices, on_device(): lax.all_gather(rim, 'chan', axis=0, tiled=True)  43.9 us
    dot_general x26, matrix products, conv_taps(): jnp.einsum('oc,chw->ohw', taps, window, preferred_element_type=jnp.float32)  33.9 us
    scatter-add x1, other arithmetic, on_device(): sums = jax.ops.segment_sum(share.T, mine, num_segments=owners * basins_here)  30.7 us
    dynamic_update_slice x30, other arithmetic, bucket_run(): final, runoff = lax.scan(day, start, (precip, temp, pet))  22.6 us
    sub x30, other arithmetic, day(): lower = lower - base  21.8 us
    all_to_all x1, waiting for transfers between devices, on_device(): lax.all_to_all(sums, 'tile', split_axis=1, concat_axis=1, tiled=True)  12.6 us
    reduce_scatter x1, waiting for transfers between devices, on_device(): lax.psum_scatter(jnp.einsum('cp,chw->hpw', head_weight, hidden, preferred...  12.1 us
    ppermute x3, starting transfers between devices, padded_2(): lax.ppermute(tail, axis, [(i, (i + 1) % count) for i in range(ends)])  10.5 us
  transfers between devices with their start and end apart: 10, of which 7 were waited for; matrix products, arithmetic and copies ran while one was open for 1% of the time, Pallas kernels for 0%

commit v1 on v0

--- a/solution.py
+++ b/solution.py
@@ -116,9 +116,14 @@
     hidden = jnp.maximum(first, 0.0).astype(jnp.bfloat16)
     for weight in (conv_second, conv_third):
         rim = padded_2(hidden, (("tile", 1),), 1)
-        total = conv_taps(
-            empty, weight, pad_columns(lax.all_gather(rim, "chan", axis=0, tiled=True))
-        )
+
+        def recast_joints(u):
+            side_arr = lax.all_to_all(
+                jnp.stack([u] * lax.axis_size("chan")), "chan", split_axis=0, concat_axis=0
+            )
+            return jnp.concatenate(side_arr, 0)
+
+        total = conv_taps(empty, weight, pad_columns(recast_joints(rim)))
         hidden = jnp.maximum(total, 0.0).astype(jnp.bfloat16)
     raw = lax.psum_scatter(
         jnp.einsum("cp,chw->hpw", head_weight, hidden, preferred_element_type=jnp.float32),

time: 259 us -> 236 us (0.911)
  waiting for transfers between devices: 77.8 us -> 41.6 us
  blocking collectives: 3.81 us -> 19.5 us
  matrix products: 46.1 us -> 42.8 us
    all_gather x2 -> x0, waiting for transfers between devices: 43.9 us -> none  [on_device(): lax.all_gather(rim, 'chan', axis=0, tiled=True)]
    all_to_all x0 -> x2, blocking collectives: none -> 15.7 us  [recast_joints(): lax.all_to_all(jnp.stack([u] * lax.axis_size('chan')), 'chan', split_axis...]
    reduce_scatter x1, waiting for transfers between devices: 12.1 us -> 19.5 us  [on_device(): lax.psum_scatter(jnp.einsum('cp,chw->hpw', head_weight, hidden, preferred...]
    dot_general x26, matrix products: 33.9 us -> 30.5 us  [conv_taps(): jnp.einsum('oc,chw->ohw', taps, window, preferred_element_type=jnp.float32)]
  transfers between devices with their start and end apart: 10 -> 8, of which waited for: 7 -> 5; matrix products, arithmetic and copies ran while one was open for 1% -> 1% of each run, Pallas kernels for 0% -> 0%
where the time goes in v1:
time: 236 us; the launch traced here: 233 us
  other arithmetic  77.6 us (33%)
  matrix products  42.8 us (18%)
  waiting for transfers between devices  41.6 us (18%)
  starting transfers between devices  25.9 us (11%)
  blocking collectives  19.5 us (8%)
  between operations  13.8 us (6%)
  local copies, waits for them, and re-layouts  10.8 us (5%)
    scatter-add x1, other arithmetic, on_device(): sums = jax.ops.segment_sum(share.T, mine, num_segments=owners * basins_here)  30.7 us
    dot_general x26, matrix products, conv_taps(): jnp.einsum('oc,chw->ohw', taps, window, preferred_element_type=jnp.float32)  30.5 us
    dynamic_update_slice x30, other arithmetic, bucket_run(): final, runoff = lax.scan(day, start, (precip, temp, pet))  22.6 us
    sub x30, other arithmetic, day(): lower = lower - base  21.8 us
    reduce_scatter x1, waiting for transfers between devices, on_device(): lax.psum_scatter(jnp.einsum('cp,chw->hpw', head_weight, hidden, preferred...  19.5 us
    all_to_all x2, blocking collectives, recast_joints(): lax.all_to_all(jnp.stack([u] * lax.axis_size('chan')), 'chan', split_axis...  15.7 us
    all_to_all x1, waiting for transfers between devices, on_device(): lax.all_to_all(sums, 'tile', split_axis=1, concat_axis=1, tiled=True)  12.7 us
    ppermute x3, starting transfers between devices, padded_2(): lax.ppermute(tail, axis, [(i, (i + 1) % count) for i in range(ends)])  11.8 us
  transfers between devices with their start and end apart: 8, of which 5 were waited for; matrix products, arithmetic and copies ran while one was open for 1% of the time, Pallas kernels for 0%

profile of v1, /device:TPU:1, one launch (start us, length us, event | category | flops | bytes accessed | tf_op | source)
XLA Modules:
  0.0 232.7 jit_solution(14305704264631995043)
XLA Ops:
  6.5 1.4 copy.83
  7.9 3.9 %collective-permute-start = (bf16[35,1,512]{2,0,1:T(8,128)(2,1)S(1)}, bf16[35,1,512]{2,0,1:T(8,128)(2,1)S(1)}, u32[]{:S(2)}, u32[]{:S(2)}) collective-permute-start(bf16[35,1,512]{2,0,1:T(8,128)(2,1)S(1)} %get-tuple-element.376), channel_id=1, source_target_pairs={{0,2},{2,4},{4,6},{6,8},{8,10},{10,12},{12,14},{14,16},{16,18},{18... | collective-permute-start | bytes 107528 | tf_op jit(solution)/shard_map/ppermute | solution.py:19
  11.9 1.4 collective-permute-start.1
  13.3 1.7 fusion.125
  15.1 1.7 collective-permute-done.1
  20.9 2.4 %fusion.36 = bf16[64,16,512]{2,0,1:T(8,128)(2,1)S(1)} fusion(f32[16,512,64]{1,2,0:T(8,128)S(1)} %fusion.66, f32[16,512,64]{1,2,0:T(8,128)S(1)} %fusion.71, f32[16,512,64]{1,2,0:T(8,128)S(1)} %fusion.73, f32[64,16,512]{2,0,1:T(8,128)S(1)} %fusion.125, f32[16,512,64]{1,2,0:T(8,128)S(1)} %fusion.75, f32[16,512,64]{1,2,0:T(8,128)S(1)} %fusion.77, ...), kind=kOutput, calls=%fused_computation.71 | convolution fusion | flops 41943040 | bytes 18491392 | tf_op jit(solution)/shard_map/oc,chw->ohw/dot_general | solution.py:39
  23.3 3.1 %collective-permute-start.2 = (bf16[64,1,512]{2,0,1:T(8,128)(2,1)S(1)}, bf16[64,1,512]{2,0,1:T(8,128)(2,1)S(1)}, u32[]{:S(2)}, u32[]{:S(2)}) collective-permute-start(bf16[64,1,512]{2,0,1:T(8,128)(2,1)S(1)} %get-tuple-element.374), channel_id=1, source_target_pairs={{0,2},{2,4},{4,6},{6,8},{8,10},{10,12},{12,14},{14,16},{16,18},{18... | collective-permute-start | bytes 196616 | tf_op jit(solution)/shard_map/ppermute | solution.py:19
  26.4 1.3 collective-permute-start.3
  27.7 3.7 %collective-permute-done.3 = bf16[64,1,512]{2,0,1:T(8,128)(2,1)S(1)} collective-permute-done((bf16[64,1,512]{2,0,1:T(8,128)(2,1)S(1)}, bf16[64,1,512]{2,0,1:T(8,128)(2,1)S(1)}, u32[]{:S(2)}, u32[]{:S(2)}) %collective-permute-start.3) | collective-permute-done | bytes 65568 | tf_op jit(solution)/shard_map/ppermute | solution.py:21
  31.8 8.9 %all_to_all.15 = bf16[2,64,18,512]{3,1,2,0:T(8,128)(2,1)S(1)} all-to-all(bf16[2,64,18,512]{3,1,2,0:T(8,128)(2,1)S(1)} %pad_maximum_fusion), channel_id=1, replica_groups=mesh['tile'=64,'chan'=2] {'chan'}, dimensions={0} | all-to-all | bytes 4718592 | tf_op jit(solution)/shard_map/all_to_all | solution.py:121
  40.8 0.8 copy-done.2
  41.6 0.8 fusion.11
  42.4 0.8 fusion.12
  43.1 0.8 fusion.13
  43.9 0.8 fusion.14
  44.7 0.8 fusion.15
  45.5 0.8 fusion.16
  47.2 1.1 fusion.44
  48.3 4.8 %collective-permute-start.4 = (bf16[64,1,512]{2,0,1:T(8,128)(2,1)S(1)}, bf16[64,1,512]{2,0,1:T(8,128)(2,1)S(1)}, u32[]{:S(2)}, u32[]{:S(2)}) collective-permute-start(bf16[64,1,512]{2,0,1:T(8,128)(2,1)S(1)} %get-tuple-element.372), channel_id=1, source_target_pairs={{0,2},{2,4},{4,6},{6,8},{8,10},{10,12},{12,14},{14,16},{16,18},{18... | collective-permute-start | bytes 196616 | tf_op jit(solution)/shard_map/ppermute | solution.py:19
  53.0 1.3 collective-permute-start.5
  54.4 4.0 %collective-permute-done.5 = bf16[64,1,512]{2,0,1:T(8,128)(2,1)S(1)} collective-permute-done((bf16[64,1,512]{2,0,1:T(8,128)(2,1)S(1)}, bf16[64,1,512]{2,0,1:T(8,128)(2,1)S(1)}, u32[]{:S(2)}, u32[]{:S(2)}) %collective-permute-start.5) | collective-permute-done | bytes 65568 | tf_op jit(solution)/shard_map/ppermute | solution.py:21
  58.7 6.8 %all_to_all.16 = bf16[2,64,18,512]{3,1,2,0:T(8,128)(2,1)S(1)} all-to-all(bf16[2,64,18,512]{3,1,2,0:T(8,128)(2,1)S(1)} %pad_maximum_fusion.1), channel_id=1, replica_groups=mesh['tile'=64,'chan'=2] {'chan'}, dimensions={0} | all-to-all | bytes 4718592 | tf_op jit(solution)/shard_map/all_to_all | solution.py:121
  66.4 2.1 fusion.17
  68.5 2.1 fusion.18
  70.6 2.1 fusion.19
  72.7 2.1 fusion.20
  74.9 2.1 fusion.21
  77.0 2.1 fusion.22
  79.1 1.7 fusion.23
  80.8 1.8 fusion.25
  82.6 8.2 %fusion.53 = f32[16,12,512]{2,1,0:T(8,128)} fusion(f32[16,512,64]{1,2,0:T(8,128)} %fusion.22, f32[16,512,64]{1,2,0:T(8,128)} %fusion.23, f32[16,512,64]{1,2,0:T(8,128)} %fusion.21, f32[16,512,64]{1,2,0:T(8,128)} %fusion.20, f32[16,512,64]{1,2,0:T(8,128)} %fusion.25, f32[16,512,64]{1,2,0:T(8,128)} %fusion.19, f32[16,512,64]{1,2,0:T(8,128)} %fusion.18, ...), kind=kOutput, calls=%fused_computation.85 | convolution fusion | flops 152043520 | bytes 19288064 | tf_op jit(solution)/shard_map/cp,chw->hpw/dot_general | solution.py:129
  91.0 19.5 %reduce-scatter.2.cloned.1.call-done = f32[8,12,512]{2,1,0:T(8,128)} async-done(((f32[16,12,512]{2,1,0:T(8,128)}), f32[8,12,512]{2,1,0:T(8,128)}) %reduce-scatter.2.cloned.1.call-update) | async-done | bytes 196624 | tf_op jit(solution)/shard_map/reduce_scatter | solution.py:128
  110.5 1.0 divide_bitcast_fusion
  112.5 30.7 %scatter_custom_fusion = f32[8192,12]{1,0:T(8,128)} fusion(s32[4096]{0:T(1024)S(1)} %bitcast.313, f32[4096,12]{1,0:T(8,128)S(1)} %copy.92, f32[]{:T(128)} %constant.50.clone.1), kind=kCustom, calls=%fused_computation.78 | custom fusion | flops 49152 | bytes 393220 | tf_op jit(solution)/shard_map/scatter-add | solution.py:138
  143.2 3.6 %copy.93 = f32[12,64,128]{2,0,1:T(8,128)} copy(f32[12,64,128]{0,2,1:T(8,128)} %bitcast.293) | data formatting | bytes 786432 | tf_op jit(solution)/shard_map/reshape | solution.py:139
  146.8 10.1 %all-to-all-start.2 = ((f32[12,64,128]{2,0,1:T(8,128)}), f32[12,64,128]{2,0,1:T(8,128)S(1)}, u32[]{:S(2)}, u32[]{:S(2)}) async-start(f32[12,64,128]{2,0,1:T(8,128)} %copy.93), calls=%async_computation.3 | async-start | bytes 1048576 | tf_op jit(solution)/shard_map/all_to_all | solution.py:140
  157.0 12.7 %all-to-all-done.2 = f32[12,64,128]{2,0,1:T(8,128)S(1)} async-done(((f32[12,64,128]{2,0,1:T(8,128)}), f32[12,64,128]{2,0,1:T(8,128)S(1)}, u32[]{:S(2)}, u32[]{:S(2)}) %all-to-all-start.2) | async-done | bytes 393248 | tf_op jit(solution)/shard_map/all_to_all | solution.py:140
  169.8 3.8 %psum.7 = f32[12,128]{1,0:T(8,128)S(1)} all-reduce(f32[12,128]{1,0:T(8,128)S(1)} %reduce_sum.18), channel_id=1, replica_groups=mesh['tile'=64,'chan'=2] {'chan'}, use_global_device_ids=true, to_apply=%region_3.4 | all-reduce | flops 1536 | bytes 12288 | tf_op jit(solution)/shard_map/psum | solution.py:142
  174.4 1.9 copy.97
  176.3 45.1 %while.21 = (s32[]{:T(128)}, f32[8,128]{1,0:T(8,128)S(1)}, f32[8,128]{1,0:T(8,128)S(1)}, f32[8,128]{1,0:T(8,128)S(1)}, f32[8,128]{1,0:T(8,128)S(1)}, /*index=5*/...) while((s32[]{:T(128)}, f32[8,128]{1,0:T(8,128)S(1)}, ...), condition=%wide.region_5.6_spmd.clone, body=%wide.region_4.5_spmd.clone.sunk | while | flops 63491 | bytes 82640 | solution.py:79
  200.3 0.8 fusion.177
  201.8 0.8 fusion.177
  203.3 0.8 fusion.177
  207.8 0.8 fusion.177
  209.4 0.8 fusion.177
  210.9 0.8 fusion.177
  221.6 3.4 %convolution_bitcast_fusion = f32[30,8,128]{0,1,2:T(8,128)S(1)} fusion(f32[30,8,128]{0,1,2:T(8,128)S(1)} %copy.96, f32[30,30,128]{1,0,2:T(8,128)S(1)} %copy.97), kind=kOutput, calls=%fused_computation.84 | convolution fusion | flops 11059200 | bytes 706560 | tf_op jit(solution)/shard_map/tsb,swb->twb/dot_general | solution.py:93
  225.0 0.9 copy.98
  (114 shorter events, 48.7 us)
Async XLA Ops:
  6.5 84.4 %copy-start = (s32[16,512]{1,0:T(8,128)S(1)}, s32[16,512]{1,0:T(8,128)}, u32[]{:S(2)}) copy-start(s32[16,512]{1,0:T(8,128)} %param.15) | copy-start | bytes 98308
  6.5 103.9 %reduce-scatter.2.cloned.1.call-start = ((), (), s32[]{:S(2)}) async-start(), calls=%async_computation.4 | async-start | bytes 786432 | tf_op jit(solution)/shard_map/reduce_scatter | solution.py:128
  7.9 7.1 %collective-permute-start = (bf16[35,1,512]{2,0,1:T(8,128)(2,1)S(1)}, bf16[35,1,512]{2,0,1:T(8,128)(2,1)S(1)}, u32[]{:S(2)}, u32[]{:S(2)}) collective-permute-start(bf16[35,1,512]{2,0,1:T(8,128)(2,1)S(1)} %get-tuple-element.376), channel_id=1, source_target_pairs={{0,2},{2,4},{4,6},{6,8},{8,10},{10,12},{12,14},{14,16},{16,18},{18... | collective-permute-start | bytes 107528 | tf_op jit(solution)/shard_map/ppermute | solution.py:19
  11.9 5.4 %copy-start.3 = (bf16[64,3,3,35]{0,3,2,1:T(8,128)(2,1)S(1)}, bf16[64,3,3,35]{0,3,2,1:T(8,128)(2,1)}, u32[]{:S(2)}) copy-start(bf16[64,3,3,35]{0,3,2,1:T(8,128)(2,1)} %param.17) | copy-start | bytes 120964
  11.9 4.9 %collective-permute-start.1 = (bf16[35,1,512]{2,0,1:T(8,128)(2,1)S(1)}, bf16[35,1,512]{2,0,1:T(8,128)(2,1)S(1)}, u32[]{:S(2)}, u32[]{:S(2)}) collective-permute-start(bf16[35,1,512]{2,0,1:T(8,128)(2,1)S(1)} %get-tuple-element.377), channel_id=1, source_target_pairs={{2,0},{4,2},{6,4},{8,6},{10,8},{12,10},{14,12},{16,14},{18,16},{20... | collective-permute-start | bytes 107528 | tf_op jit(solution)/shard_map/ppermute | solution.py:21
  23.3 4.4 %collective-permute-start.2 = (bf16[64,1,512]{2,0,1:T(8,128)(2,1)S(1)}, bf16[64,1,512]{2,0,1:T(8,128)(2,1)S(1)}, u32[]{:S(2)}, u32[]{:S(2)}) collective-permute-start(bf16[64,1,512]{2,0,1:T(8,128)(2,1)S(1)} %get-tuple-element.374), channel_id=1, source_target_pairs={{0,2},{2,4},{4,6},{6,8},{8,10},{10,12},{12,14},{14,16},{16,18},{18... | collective-permute-start | bytes 196616 | tf_op jit(solution)/shard_map/ppermute | solution.py:19
  26.4 5.0 %collective-permute-start.3 = (bf16[64,1,512]{2,0,1:T(8,128)(2,1)S(1)}, bf16[64,1,512]{2,0,1:T(8,128)(2,1)S(1)}, u32[]{:S(2)}, u32[]{:S(2)}) collective-permute-start(bf16[64,1,512]{2,0,1:T(8,128)(2,1)S(1)} %get-tuple-element.375), channel_id=1, source_target_pairs={{2,0},{4,2},{6,4},{8,6},{10,8},{12,10},{14,12},{16,14},{18,16},{20... | collective-permute-start | bytes 196616 | tf_op jit(solution)/shard_map/ppermute | solution.py:21
  40.7 0.9 copy-start.2
  48.3 6.1 %collective-permute-start.4 = (bf16[64,1,512]{2,0,1:T(8,128)(2,1)S(1)}, bf16[64,1,512]{2,0,1:T(8,128)(2,1)S(1)}, u32[]{:S(2)}, u32[]{:S(2)}) collective-permute-start(bf16[64,1,512]{2,0,1:T(8,128)(2,1)S(1)} %get-tuple-element.372), channel_id=1, source_target_pairs={{0,2},{2,4},{4,6},{6,8},{8,10},{10,12},{12,14},{14,16},{16,18},{18... | collective-permute-start | bytes 196616 | tf_op jit(solution)/shard_map/ppermute | solution.py:19
  53.0 5.3 %collective-permute-start.5 = (bf16[64,1,512]{2,0,1:T(8,128)(2,1)S(1)}, bf16[64,1,512]{2,0,1:T(8,128)(2,1)S(1)}, u32[]{:S(2)}, u32[]{:S(2)}) collective-permute-start(bf16[64,1,512]{2,0,1:T(8,128)(2,1)S(1)} %get-tuple-element.373), channel_id=1, source_target_pairs={{2,0},{4,2},{6,4},{8,6},{10,8},{12,10},{14,12},{16,14},{18,16},{20... | collective-permute-start | bytes 196616 | tf_op jit(solution)/shard_map/ppermute | solution.py:21
  65.5 0.9 copy-start.1
  80.8 1.8 copy-start.4
  143.2 13.8 %copy-start.7 = (s32[128]{0:T(128)S(1)}, s32[128]{0:T(128)}, u32[]{:S(2)}) copy-start(s32[128]{0:T(128)} %param.16) | copy-start | bytes 1540
  143.2 30.3 %copy-start.5 = (f32[12]{0:T(128)S(1)}, f32[12]{0:T(128)}, u32[]{:S(2)}) copy-start(f32[12]{0:T(128)} %constant.60.clone) | copy-start | bytes 148
  143.2 30.4 %copy-start.6 = (f32[12]{0:T(128)S(1)}, f32[12]{0:T(128)}, u32[]{:S(2)}) copy-start(f32[12]{0:T(128)} %constant.61.clone) | copy-start | bytes 148
  146.8 22.9 %all-to-all-start.2 = ((f32[12,64,128]{2,0,1:T(8,128)}), f32[12,64,128]{2,0,1:T(8,128)S(1)}, u32[]{:S(2)}, u32[]{:S(2)}) async-start(f32[12,64,128]{2,0,1:T(8,128)} %copy.93), calls=%async_computation.3 | async-start | bytes 1048576 | tf_op jit(solution)/shard_map/all_to_all | solution.py:140
Sparse Core Ops, SparseCore 0:
  91.0 19.3 reduce-scatter.1
